TPU v7x, 32 devices: a whole 2x2x4 slice. The times are simulated.
32 devices in a mesh: tm: 8 (over z, x), inner: 4 (over y, core).
Axes of the slice: x: 2, y: 2, z: 4, core: 2. Of those that a mesh axis runs over, the one named last changes fastest.
Arguments:
- start_panels: float32 [8, 192, 2048], P('tm', None, 'inner'), may hold values from -6 to 6
- kinetic: float32 [2048, 2048], P('inner')
- fields: int32 [8, 2048], P('tm'), may hold values from -1 to 1, as said below
Outputs:
- orbitals: float32 [8, 4, 192, 2048], P('tm', None, None, 'inner')
- log_scales: float32 [8, 4, 192], P('tm')
Inputs may be any that keep to these rules, and one draw needn't show every extreme that they name: `fields`: each entry is -1 or +1.
All inputs are finite; a program needn't handle non-finite values.
Results may differ from a plain program's by a relative error of at most 0.0003.
Values sent between devices are 32-bit elements; how exact they have to be, the bound alone decides.
A program may use at most 128 MiB of HBM per device.

v0:
```python
import math

import jax
import jax.numpy as jnp
from jax import lax
from jax.sharding import PartitionSpec as P

coupling = 0.17725


def from_behind(block, axis, distance):
    devices = range(lax.axis_size(axis))
    route = [((i - distance) % len(devices), i) for i in devices]
    return lax.ppermute(block, axis, route)


def contract_last(left, right):
    return lax.dot_general(
        left,
        right,
        (((1,), (1,)), ((), ())),
        precision=lax.Precision.HIGHEST,
        preferred_element_type=jnp.float32,
    )


def factor_panel(panel, gram_matrix):
    lower = jnp.linalg.cholesky(gram_matrix)
    orthonormal = lax.linalg.triangular_solve(lower, panel, left_side=True, lower=True)
    return (orthonormal, jnp.log(jnp.diagonal(lower)))


def on_device(start_panels, kinetic, fields):
    rows = kinetic.shape[0]
    sites = kinetic.shape[1]
    rank = lax.axis_index("inner")
    hops = lax.axis_size("tm") // 2
    first = rank * rows
    scales = jnp.exp(coupling * fields.astype(jnp.float32))
    orbit_list = []
    log_list = []
    own_scales = lax.dynamic_slice_in_dim(scales, first, rows, 1)
    own_block = start_panels[0]
    for hop in range(hops):
        own_block = (
            contract_last(lax.all_gather(own_block, "inner", axis=1, tiled=True), kinetic)
            * own_scales[0][None, :]
        )
        gram_matrix = lax.psum(contract_last(own_block, own_block), "inner")
        own_block, log_diag = factor_panel(own_block, gram_matrix)
        orbit_list.append(math.sqrt(sites) * own_block)
        log_list.append(log_diag)
        if hop + 1 < hops:
            own_block = from_behind(own_block, "tm", 1)
    return (jnp.stack(orbit_list, 0)[None], jnp.stack(log_list, 0)[None])


def solution(mesh):
    placed = (P("tm", None, "inner"), P("inner", None), P("tm", None))
    return jax.shard_map(
        on_device,
        mesh=mesh,
        in_specs=placed,
        out_specs=(P("tm", None, None, "inner"), P("tm", None, None)),
        check_vma=False,
    )
```

profile of v0, /device:TPU:0, one launch (start us, length us, event | category | flops | bytes accessed | tf_op | source)
XLA Modules:
  0.0 507.4 jit_solution(18321025305933474092)
XLA Ops:
  7.2 0.7 all-gather.12.cloned.1.call-update
  7.9 0.7 fusion.51
  8.7 23.3 %all-gather.12.cloned.1.call-done = f32[1,192,2048]{2,1,0:T(8,128)} async-done(((f32[1,192,512]{2,1,0:T(8,128)}), f32[1,192,2048]{2,1,0:T(8,128)}) %all-gather.12.cloned.1.call-update) | async-done | bytes 1572880 | tf_op jit(solution)/shard_map/all_gather | solution.py:46
  32.0 6.6 %fusion.2 = f32[192,512]{1,0:T(8,128)S(1)} fusion(f32[512,2048]{1,0:T(8,128)} %param.7, f32[1,192,2048]{2,1,0:T(8,128)} %all-gather.12.cloned.1.call-done, f32[512]{0:T(512)S(1)} %bitcast.139), kind=kOutput, calls=%fused_computation.7 | convolution fusion | flops 2416017408 | bytes 6162432 | tf_op jit(solution)/shard_map/dot_general | solution.py:18
  38.6 1.2 fusion.53
  40.0 31.6 %all-reduce.8.cloned.1.call-done = f32[192,192]{0,1:T(8,128)} async-done(((f32[192,192]{0,1:T(8,128)}), f32[192,192]{0,1:T(8,128)}) %all-reduce.8.cloned.1.call-update) | async-done | bytes 147472 | tf_op jit(solution)/shard_map/psum | solution.py:49
  71.6 1.0 copy.14
  72.7 1.0 fusion.17
  73.6 11.7 %cholesky.228 = f32[128,128]{1,0:T(8,128)S(1)} custom-call(f32[128,128]{1,0:T(8,128)S(1)} %cholesky.376), custom_call_target="Cholesky" | custom-call | tf_op jit(solution)/shard_map/jit(cholesky)/cholesky | solution.py:28
  85.4 0.6 compare_reduce_fusion.7
  86.0 9.8 %custom-call.25 = f32[1,128,128]{1,2,0:T(8,128)S(1)} custom-call(f32[1,128,128]{2,1,0:T(8,128)S(1)} %get-tuple-element.63), custom_call_target="InvertDiagBlocksLowerTriangular" | custom-call | tf_op jit(solution)/shard_map/jit(cholesky)/cholesky | solution.py:28
  96.2 5.8 %cholesky.248 = f32[64,64]{1,0:T(8,128)S(1)} custom-call(f32[64,64]{1,0:T(8,128)S(1)} %convolution_subtract_fusion.4), custom_call_target="Cholesky" | custom-call | tf_op jit(solution)/shard_map/jit(cholesky)/cholesky | solution.py:28
  102.1 0.6 compare_reduce_fusion.6
  104.2 19.7 %custom-call.26 = f32[2,128,128]{1,2,0:T(8,128)S(1)} custom-call(f32[2,128,128]{2,1,0:T(8,128)S(1)} %pad_maximum_fusion.3), custom_call_target="InvertDiagBlocksLowerTriangular" | custom-call | tf_op jit(solution)/shard_map/triangular_solve/custom-call.0 | solution.py:29
  125.0 1.5 collective-permute-start
  126.5 10.8 %collective-permute-done = f32[192,512]{1,0:T(8,128)S(1)} collective-permute-done((f32[192,512]{1,0:T(8,128)S(1)}, f32[192,512]{1,0:T(8,128)S(1)}, u32[]{:S(2)}, u32[]{:S(2)}) %collective-permute-start) | collective-permute-done | bytes 393248 | tf_op jit(solution)/shard_map/ppermute | solution.py:14
  137.3 0.7 copy-done
  138.6 17.1 %all-gather.6.cloned.1.call-done = f32[192,2048]{1,0:T(8,128)} async-done(((f32[192,512]{1,0:T(8,128)}), f32[192,2048]{1,0:T(8,128)}) %all-gather.6.cloned.1.call-update) | async-done | bytes 1572880 | tf_op jit(solution)/shard_map/all_gather | solution.py:46
  155.7 6.6 %convolution_multiply_fusion.2 = f32[192,512]{1,0:T(8,128)S(1)} fusion(f32[192,2048]{1,0:T(8,128)} %all-gather.6.cloned.1.call-done, f32[512,2048]{1,0:T(8,128)} %param.7, f32[512]{0:T(512)S(1)} %bitcast.140), kind=kOutput, calls=%fused_computation.10 | convolution fusion | flops 2416017408 | bytes 6162432 | tf_op jit(solution)/shard_map/dot_general | solution.py:18
  162.3 1.2 fusion.54
  163.6 31.8 %all-reduce.10.cloned.1.call-done = f32[192,192]{0,1:T(8,128)} async-done(((f32[192,192]{0,1:T(8,128)}), f32[192,192]{0,1:T(8,128)}) %all-reduce.10.cloned.1.call-update) | async-done | bytes 147472 | tf_op jit(solution)/shard_map/psum | solution.py:49
  195.4 1.0 copy.16
  196.4 1.0 fusion.16
  197.4 11.7 %cholesky.266 = f32[128,128]{1,0:T(8,128)S(1)} custom-call(f32[128,128]{1,0:T(8,128)S(1)} %cholesky.379), custom_call_target="Cholesky" | custom-call | tf_op jit(solution)/shard_map/jit(cholesky)/cholesky | solution.py:28
  209.2 0.6 compare_reduce_fusion.5
  209.8 9.8 %custom-call.27 = f32[1,128,128]{1,2,0:T(8,128)S(1)} custom-call(f32[1,128,128]{2,1,0:T(8,128)S(1)} %get-tuple-element.61), custom_call_target="InvertDiagBlocksLowerTriangular" | custom-call | tf_op jit(solution)/shard_map/jit(cholesky)/cholesky | solution.py:28
  220.0 5.8 %cholesky.286 = f32[64,64]{1,0:T(8,128)S(1)} custom-call(f32[64,64]{1,0:T(8,128)S(1)} %convolution_subtract_fusion.3), custom_call_target="Cholesky" | custom-call | tf_op jit(solution)/shard_map/jit(cholesky)/cholesky | solution.py:28
  225.9 0.6 compare_reduce_fusion.4
  228.0 19.7 %custom-call.28 = f32[2,128,128]{1,2,0:T(8,128)S(1)} custom-call(f32[2,128,128]{2,1,0:T(8,128)S(1)} %pad_maximum_fusion.4), custom_call_target="InvertDiagBlocksLowerTriangular" | custom-call | tf_op jit(solution)/shard_map/triangular_solve/custom-call.0 | solution.py:29
  248.8 1.5 collective-permute-start.1
  250.3 10.8 %collective-permute-done.1 = f32[192,512]{1,0:T(8,128)S(1)} collective-permute-done((f32[192,512]{1,0:T(8,128)S(1)}, f32[192,512]{1,0:T(8,128)S(1)}, u32[]{:S(2)}, u32[]{:S(2)}) %collective-permute-start.1) | collective-permute-done | bytes 393248 | tf_op jit(solution)/shard_map/ppermute | solution.py:14
  261.1 0.7 copy-done.1
  262.1 17.3 %all-gather.8.cloned.1.call-done = f32[192,2048]{1,0:T(8,128)} async-done(((f32[192,512]{1,0:T(8,128)}), f32[192,2048]{1,0:T(8,128)}) %all-gather.8.cloned.1.call-update) | async-done | bytes 1572880 | tf_op jit(solution)/shard_map/all_gather | solution.py:46
  279.5 6.6 %convolution_multiply_fusion.1 = f32[192,512]{1,0:T(8,128)S(1)} fusion(f32[192,2048]{1,0:T(8,128)} %all-gather.8.cloned.1.call-done, f32[512,2048]{1,0:T(8,128)} %param.7, f32[512]{0:T(512)S(1)} %bitcast.141), kind=kOutput, calls=%fused_computation.9 | convolution fusion | flops 2416017408 | bytes 6162432 | tf_op jit(solution)/shard_map/dot_general | solution.py:18
  286.1 1.2 fusion.55
  287.3 31.8 %all-reduce.12.cloned.1.call-done = f32[192,192]{0,1:T(8,128)} async-done(((f32[192,192]{0,1:T(8,128)}), f32[192,192]{0,1:T(8,128)}) %all-reduce.12.cloned.1.call-update) | async-done | bytes 147472 | tf_op jit(solution)/shard_map/psum | solution.py:49
  319.1 1.0 copy.18
  320.2 1.0 fusion.15
  321.2 11.7 %cholesky.304 = f32[128,128]{1,0:T(8,128)S(1)} custom-call(f32[128,128]{1,0:T(8,128)S(1)} %cholesky.382), custom_call_target="Cholesky" | custom-call | tf_op jit(solution)/shard_map/jit(cholesky)/cholesky | solution.py:28
  332.9 0.6 compare_reduce_fusion.3
  333.6 9.8 %custom-call.29 = f32[1,128,128]{1,2,0:T(8,128)S(1)} custom-call(f32[1,128,128]{2,1,0:T(8,128)S(1)} %get-tuple-element.59), custom_call_target="InvertDiagBlocksLowerTriangular" | custom-call | tf_op jit(solution)/shard_map/jit(cholesky)/cholesky | solution.py:28
  343.8 5.8 %cholesky.324 = f32[64,64]{1,0:T(8,128)S(1)} custom-call(f32[64,64]{1,0:T(8,128)S(1)} %convolution_subtract_fusion.2), custom_call_target="Cholesky" | custom-call | tf_op jit(solution)/shard_map/jit(cholesky)/cholesky | solution.py:28
  349.6 0.6 compare_reduce_fusion.2
  351.8 19.7 %custom-call.30 = f32[2,128,128]{1,2,0:T(8,128)S(1)} custom-call(f32[2,128,128]{2,1,0:T(8,128)S(1)} %pad_maximum_fusion.5), custom_call_target="InvertDiagBlocksLowerTriangular" | custom-call | tf_op jit(solution)/shard_map/triangular_solve/custom-call.0 | solution.py:29
  372.5 1.5 collective-permute-start.2
  374.1 10.8 %collective-permute-done.2 = f32[192,512]{1,0:T(8,128)S(1)} collective-permute-done((f32[192,512]{1,0:T(8,128)S(1)}, f32[192,512]{1,0:T(8,128)S(1)}, u32[]{:S(2)}, u32[]{:S(2)}) %collective-permute-start.2) | collective-permute-done | bytes 393248 | tf_op jit(solution)/shard_map/ppermute | solution.py:14
  384.9 0.7 copy-done.2
  385.9 17.3 %all-gather.10.cloned.1.call-done = f32[192,2048]{1,0:T(8,128)} async-done(((f32[192,512]{1,0:T(8,128)}), f32[192,2048]{1,0:T(8,128)}) %all-gather.10.cloned.1.call-update) | async-done | bytes 1572880 | tf_op jit(solution)/shard_map/all_gather | solution.py:46
  403.2 6.6 %convolution_multiply_fusion = f32[192,512]{1,0:T(8,128)S(1)} fusion(f32[192,2048]{1,0:T(8,128)} %all-gather.10.cloned.1.call-done, f32[512,2048]{1,0:T(8,128)} %param.7, f32[512]{0:T(512)S(1)} %bitcast.142), kind=kOutput, calls=%fused_computation.8 | convolution fusion | flops 2416017408 | bytes 6162432 | tf_op jit(solution)/shard_map/dot_general | solution.py:18
  409.8 1.2 fusion.56
  411.1 1.9 gather_fusion
  413.0 1.9 gather_fusion.1
  414.9 1.9 gather_fusion.2
  416.8 26.0 %all-reduce.14.cloned.1.call-done = f32[192,192]{0,1:T(8,128)} async-done(((f32[192,192]{0,1:T(8,128)}), f32[192,192]{0,1:T(8,128)}) %all-reduce.14.cloned.1.call-update) | async-done | bytes 147472 | tf_op jit(solution)/shard_map/psum | solution.py:49
  442.9 1.0 copy.20
  443.9 1.0 fusion.14
  444.9 11.7 %cholesky.342 = f32[128,128]{1,0:T(8,128)S(1)} custom-call(f32[128,128]{1,0:T(8,128)S(1)} %cholesky.385), custom_call_target="Cholesky" | custom-call | tf_op jit(solution)/shard_map/jit(cholesky)/cholesky | solution.py:28
  456.7 0.6 compare_reduce_fusion.1
  457.3 9.8 %custom-call.31 = f32[1,128,128]{1,2,0:T(8,128)S(1)} custom-call(f32[1,128,128]{2,1,0:T(8,128)S(1)} %get-tuple-element.57), custom_call_target="InvertDiagBlocksLowerTriangular" | custom-call | tf_op jit(solution)/shard_map/jit(cholesky)/cholesky | solution.py:28
  467.5 5.8 %cholesky.362 = f32[64,64]{1,0:T(8,128)S(1)} custom-call(f32[64,64]{1,0:T(8,128)S(1)} %convolution_subtract_fusion.1), custom_call_target="Cholesky" | custom-call | tf_op jit(solution)/shard_map/jit(cholesky)/cholesky | solution.py:28
  473.4 0.6 compare_reduce_fusion
  475.4 1.9 gather_fusion.3
  477.4 19.9 %custom-call.32 = f32[2,128,128]{1,2,0:T(8,128)S(1)} custom-call(f32[2,128,128]{2,1,0:T(8,128)S(1)} %pad_maximum_fusion.6), custom_call_target="InvertDiagBlocksLowerTriangular" | custom-call | tf_op jit(solution)/shard_map/triangular_solve/custom-call.0 | solution.py:29
  499.0 1.3 maximum_bitcast_fusion
  (85 shorter events, 8.6 us)
Async XLA Ops:
  7.2 24.8 %all-gather.12.cloned.1.call-start = ((), (), s32[]{:S(2)}) async-start(), calls=%async_computation.7 | async-start | bytes 1966080 | tf_op jit(solution)/shard_map/all_gather | solution.py:46
  7.9 63.7 %all-reduce.8.cloned.1.call-start = ((), (), s32[]{:S(2)}) async-start(), calls=%async_computation | async-start | bytes 393216 | tf_op jit(solution)/shard_map/psum | solution.py:49
  39.8 115.9 %all-gather.6.cloned.1.call-start = ((), (), s32[]{:S(2)}) async-start(), calls=%async_computation.1 | async-start | bytes 1966080 | tf_op jit(solution)/shard_map/all_gather | solution.py:46
  125.0 12.3 %collective-permute-start = (f32[192,512]{1,0:T(8,128)S(1)}, f32[192,512]{1,0:T(8,128)S(1)}, u32[]{:S(2)}, u32[]{:S(2)}) collective-permute-start(f32[192,512]{1,0:T(8,128)S(1)} %get-tuple-element.51), channel_id=1, source_target_pairs={{28,0},{0,4},{4,8},{8,12},{12,16},{16,20},{20,24},{24,28},{29,1},{... | collective-permute-start | bytes 1179656 | tf_op jit(solution)/shard_map/ppermute | solution.py:14
  137.3 0.7 copy-start
  138.1 57.3 %all-reduce.10.cloned.1.call-start = ((), (), s32[]{:S(2)}) async-start(), calls=%async_computation.2 | async-start | bytes 393216 | tf_op jit(solution)/shard_map/psum | solution.py:49
  163.5 115.9 %all-gather.8.cloned.1.call-start = ((), (), s32[]{:S(2)}) async-start(), calls=%async_computation.3 | async-start | bytes 1966080 | tf_op jit(solution)/shard_map/all_gather | solution.py:46
  248.8 12.3 %collective-permute-start.1 = (f32[192,512]{1,0:T(8,128)S(1)}, f32[192,512]{1,0:T(8,128)S(1)}, u32[]{:S(2)}, u32[]{:S(2)}) collective-permute-start(f32[192,512]{1,0:T(8,128)S(1)} %get-tuple-element.53), channel_id=1, source_target_pairs={{28,0},{0,4},{4,8},{8,12},{12,16},{16,20},{20,24},{24,28},{29,1},{... | collective-permute-start | bytes 1179656 | tf_op jit(solution)/shard_map/ppermute | solution.py:14
  261.1 0.7 copy-start.1
  261.9 57.3 %all-reduce.12.cloned.1.call-start = ((), (), s32[]{:S(2)}) async-start(), calls=%async_computation.4 | async-start | bytes 393216 | tf_op jit(solution)/shard_map/psum | solution.py:49
  287.3 115.9 %all-gather.10.cloned.1.call-start = ((), (), s32[]{:S(2)}) async-start(), calls=%async_computation.5 | async-start | bytes 1966080 | tf_op jit(solution)/shard_map/all_gather | solution.py:46
  372.5 12.4 %collective-permute-start.2 = (f32[192,512]{1,0:T(8,128)S(1)}, f32[192,512]{1,0:T(8,128)S(1)}, u32[]{:S(2)}, u32[]{:S(2)}) collective-permute-start(f32[192,512]{1,0:T(8,128)S(1)} %get-tuple-element.55), channel_id=1, source_target_pairs={{28,0},{0,4},{4,8},{8,12},{12,16},{16,20},{20,24},{24,28},{29,1},{... | collective-permute-start | bytes 1179656 | tf_op jit(solution)/shard_map/ppermute | solution.py:14
  384.9 0.7 copy-start.2
  385.7 57.2 %all-reduce.14.cloned.1.call-start = ((), (), s32[]{:S(2)}) async-start(), calls=%async_computation.6 | async-start | bytes 393216 | tf_op jit(solution)/shard_map/psum | solution.py:49
Sparse Core Ops, SparseCore 0:
  9.6 22.3 all-gather.11
  39.9 31.6 all-reduce.7
  138.2 17.4 all-gather.5
  163.6 31.7 all-reduce.9
  262.0 17.4 all-gather.7
  287.4 31.6 all-reduce.11
  385.8 17.4 all-gather.9
  411.2 31.6 all-reduce.13
where the time goes:
time: 510 us; the launch traced here: 507 us
  waiting for transfers between devices  230 us (45%)
  other arithmetic  201 us (39%)
  matrix products  36.7 us (7%)
  between operations  20.3 us (4%)
  local copies, waits for them, and re-layouts  14.2 us (3%)
  starting transfers between devices  5.85 us (1%)
    psum x4, waiting for transfers between devices, on_device(): gram_matrix = lax.psum(contract_last(own_block, own_block), 'inner')  121 us
    another operation x28, other arithmetic, factor_panel(): lower = jnp.linalg.cholesky(gram_matrix)  115 us
    another operation x18, other arithmetic, factor_panel(): lax.linalg.triangular_solve(lower, panel, left_side=True, lower=True)  79.5 us
    all_gather x4, waiting for transfers between devices, on_device(): lax.all_gather(own_block, 'inner', axis=1, tiled=True)  75.1 us
    ppermute x3, waiting for transfers between devices, from_behind(): return lax.ppermute(block, axis, route)  32.5 us
    dot_general x8, matrix products, contract_last(): lax.dot_general(left, right, (((1,), (1,)), ((), ())), precision=lax.Prec...  31.2 us
  transfers between devices with their start and end apart: 11, of which 11 were waited for; matrix products, arithmetic and copies ran while one was open for 1% of the time, Pallas kernels for 0%

commit v1 on v0

v1 whole, which is shorter than its diff:
```python
import functools
import math

import jax
import jax.numpy as jnp
from jax import lax
from jax.experimental import pallas as pl
from jax.experimental.pallas import tpu as pltpu
from jax.sharding import PartitionSpec as P

coupling = 0.17725
LANES = 128
B = 8


def from_behind(block, axis, distance):
    n = lax.axis_size(axis)
    distance %= n
    if distance == 0:
        return block
    return lax.ppermute(block, axis, [((i - distance) % n, i) for i in range(n)])


def contract(left, right, dims, precision):
    return lax.dot_general(
        left,
        right,
        (dims, ((), ())),
        precision=precision,
        preferred_element_type=jnp.float32,
    )


HIGHEST = lax.Precision.HIGHEST


def factor_into(work, columns):
    r, width = work.shape
    tiles = width // LANES
    lane = lax.broadcasted_iota(jnp.int32, (1, LANES), 1)
    lane_all = lax.broadcasted_iota(jnp.int32, (1, width), 1)
    diagonal = [jnp.ones((1, LANES), jnp.float32) for _ in range(tiles)]
    for p in range(0, r, B):
        home, off = p // LANES, p % LANES
        block = work[p : p + B, home * LANES : (home + 1) * LANES]
        for j in range(B):
            columns[j * B : (j + 1) * B, :] = jnp.broadcast_to(
                block[:, off + j : off + j + 1], (B, LANES)
            )
        d = [[columns[j * B + i : j * B + i + 1, :] for j in range(i + 1)] for i in range(B)]
        rows = []
        for t in range(B):
            parts = [work[p + t : p + t + 1, q * LANES : (q + 1) * LANES] for q in range(tiles)]
            unit = (lane == off + t).astype(jnp.float32)
            parts[home] = jnp.where((lane >= off) & (lane < off + B), unit, parts[home])
            rows.append(parts)
        for t in range(B):
            inverse = lax.rsqrt(d[t][t])
            diagonal[home] = jnp.where(lane == off + t, inverse, diagonal[home])
            below = [d[s][t] * inverse for s in range(t + 1, B)]
            for s in range(t + 1, B):
                for u in range(t + 1, s + 1):
                    d[s][u] = d[s][u] - below[s - t - 1] * below[u - t - 1]
            rows[t] = [part * inverse for part in rows[t]]
            for s in range(t + 1, B):
                rows[s] = [a - below[s - t - 1] * b for a, b in zip(rows[s], rows[t])]
        for t in range(B):
            for q in range(tiles):
                work[p + t : p + t + 1, q * LANES : (q + 1) * LANES] = rows[t][q]
        if p + B < r:
            pivot = work[p : p + B, :]
            turned = pivot.T[p + B : r, :]
            change = contract(turned, pivot, ((1,), (0,)), HIGHEST)
            rest = work[p + B : r, :]
            rest = jnp.where((lane_all >= p) & (lane_all < p + B), 0.0, rest)
            work[p + B : r, :] = rest - change
    return jnp.concatenate(diagonal, axis=1)


def factor_kernel(gram, inverse, logs, work, columns):
    r = gram.shape[0]
    work[...] = jnp.zeros_like(work)
    work[:, :r] = gram[...]
    diagonal = factor_into(work, columns)
    logs[...] = -jnp.log(diagonal[:, :r])
    below = lax.broadcasted_iota(jnp.int32, (r, r), 0) >= lax.broadcasted_iota(
        jnp.int32, (r, r), 1
    )
    inverse[...] = jnp.where(below, work[:, :r], 0.0)


def factor(gram):
    r = gram.shape[0]
    width = -(-r // LANES) * LANES
    return pl.pallas_call(
        factor_kernel,
        out_shape=(
            jax.ShapeDtypeStruct((r, r), jnp.float32),
            jax.ShapeDtypeStruct((1, r), jnp.float32),
        ),
        in_specs=[pl.BlockSpec(memory_space=pltpu.VMEM)],
        out_specs=(pl.BlockSpec(memory_space=pltpu.VMEM),) * 2,
        scratch_shapes=[
            pltpu.VMEM((r, width), jnp.float32),
            pltpu.VMEM((B * B, LANES), jnp.float32),
        ],
        compiler_params=pltpu.CompilerParams(vmem_limit_bytes=16 * 2**20),
        cost_estimate=pl.CostEstimate(
            flops=10**10, bytes_accessed=3 * 4 * r * r, transcendentals=2 * r
        ),
        name="factor",
    )(gram)


def on_device(start_panels, kinetic, fields):
    rows, sites = kinetic.shape
    r = start_panels.shape[1]
    rank = lax.axis_index("inner")
    hops = lax.axis_size("tm") // 2
    first = rank * rows
    own_fields = lax.dynamic_slice_in_dim(fields, first, rows, 1)

    def mapped(panel, hop):
        scale = jnp.exp(coupling * from_behind(own_fields, "tm", -hop).astype(jnp.float32))
        return contract(panel, kinetic, ((1,), (1,)), lax.Precision.HIGH) * scale

    def gathered(block):
        return lax.all_gather(block, "inner", axis=1, tiled=True)

    def own(panel):
        return lax.dynamic_slice_in_dim(panel, first, rows, 1)

    gain = math.sqrt(sites)
    orbit_list, log_list = [], []
    panel = gathered(mapped(gathered(start_panels[0]), 0))
    for hop in range(hops):
        gram = contract(panel, panel, ((1,), (1,)), HIGHEST)
        if hop + 1 < hops:
            ahead = gathered(mapped(panel, hop + 1))
            inverse, logs = factor(gram)
            out = contract(gain * inverse, own(panel), ((1,), (0,)), HIGHEST)
            orbit_list.append(from_behind(out, "tm", hop))
            log_list.append(from_behind(logs, "tm", hop))
            panel = contract(inverse, ahead, ((1,), (0,)), HIGHEST)
        else:
            moved = from_behind(own(panel), "tm", hop)
            inverse, logs = factor(from_behind(gram, "tm", hop))
            orbit_list.append(contract(gain * inverse, moved, ((1,), (0,)), HIGHEST))
            log_list.append(logs)
    return (
        jnp.stack(orbit_list, 0)[None],
        jnp.concatenate(log_list, 0)[None],
    )


def solution(mesh):
    placed = (P("tm", None, "inner"), P("inner", None), P("tm", None))
    return jax.shard_map(
        on_device,
        mesh=mesh,
        in_specs=placed,
        out_specs=(P("tm", None, None, "inner"), P("tm", None, None)),
        check_vma=False,
    )
```

time: 510 us -> 198 us (0.39)
  other arithmetic: 201 us -> 2.62 us
  waiting for transfers between devices: 230 us -> 71 us
  Pallas kernels: 0 us -> 45.3 us
  starting transfers between devices: 5.85 us -> 20.7 us
  local copies, waits for them, and re-layouts: 14.2 us -> 0.03 us
  between operations: 20.3 us -> 14.2 us
    another operation x50 -> x0, other arithmetic: 194 us -> none  [the longest x28 115 us: factor_panel(): lower = jnp.linalg.cholesky(gram_matrix)]
    psum x4 -> x0, waiting for transfers between devices: 121 us -> none  [on_device(): gram_matrix = lax.psum(contract_last(own_block, own_block), 'inner')]
    pallas_call x0 -> x4, Pallas kernels: none -> 45.3 us  [factor(): pl.pallas_call(factor_kernel, out_shape=(jax.ShapeDtypeStruct((r, r), jnp...]
    all_gather x4 -> x5, waiting for transfers between devices: 75.1 us -> 42 us  [gathered(): return lax.all_gather(block, 'inner', axis=1, tiled=True)]
    ppermute x3 -> x9, starting transfers between devices: 4.56 us -> 20.5 us  [from_behind(): lax.ppermute(block, axis, [((i - distance) % n, i) for i in range(n)])]
    dot_general x8 -> x15, matrix products: 31.2 us -> 40.5 us  [contract(): lax.dot_general(left, right, (dims, ((), ())), precision=precision, prefe...]
    gather x4 -> x0, local copies, waits for them, and re-layouts: 7.63 us -> none  [factor_panel(): return (orthonormal, jnp.log(jnp.diagonal(lower)))]
    another operation x20 -> x0, matrix products: 5.5 us -> none  [the longest x12 4.02 us: factor_panel(): lax.linalg.triangular_solve(lower, panel, left_side=True, lower=True)]
  transfers between devices with their start and end apart: 11 -> 14, of which waited for: 11 -> 10; matrix products, arithmetic and copies ran while one was open for 1% -> 7% of each run, Pallas kernels for 0% -> 23%
where the time goes in v1:
time: 198 us; the launch traced here: 194 us
  waiting for transfers between devices  71 us (36%)
  Pallas kernels  45.3 us (23%)
  matrix products  40.5 us (20%)
  starting transfers between devices  20.7 us (10%)
  between operations  14.2 us (7%)
  other arithmetic  2.62 us (1%)
    pallas_call x4, Pallas kernels, factor(): pl.pallas_call(factor_kernel, out_shape=(jax.ShapeDtypeStruct((r, r), jnp...  45.3 us
    all_gather x5, waiting for transfers between devices, gathered(): return lax.all_gather(block, 'inner', axis=1, tiled=True)  42 us
    dot_general x15, matrix products, contract(): lax.dot_general(left, right, (dims, ((), ())), precision=precision, prefe...  40.5 us
    ppermute x9, waiting for transfers between devices, from_behind(): lax.ppermute(block, axis, [((i - distance) % n, i) for i in range(n)])  28.3 us
    ppermute x9, starting transfers between devices, from_behind(): lax.ppermute(block, axis, [((i - distance) % n, i) for i in range(n)])  20.5 us
  transfers between devices with their start and end apart: 14, of which 10 were waited for; matrix products, arithmetic and copies ran while one was open for 7% of the time, Pallas kernels for 23%

profile of v1, /device:TPU:0, one launch (start us, length us, event | category | flops | bytes accessed | tf_op | source)
XLA Modules:
  0.0 194.3 jit_solution(180247870869866696)
XLA Ops:
  7.2 0.0 all-gather.15.cloned.1.call-start
  7.2 0.7 all-gather.15.cloned.1.call-update
  7.9 0.0 all-gather.7.cloned.1.call-start
  7.9 0.7 multiply_exponential_fusion.3
  8.6 23.3 %all-gather.15.cloned.1.call-done = f32[1,192,2048]{2,1,0:T(8,128)} async-done(((f32[1,192,512]{2,1,0:T(8,128)}), f32[1,192,2048]{2,1,0:T(8,128)}) %all-gather.15.cloned.1.call-update) | async-done | bytes 1572880 | tf_op jit(solution)/shard_map/all_gather | solution.py:128
  32.0 5.6 %fusion.2 = f32[192,512]{1,0:T(8,128)} fusion(f32[512,2048]{1,0:T(8,128)} %param.4, f32[1,192,2048]{2,1,0:T(8,128)} %all-gather.15.cloned.1.call-done, f32[512]{0:T(512)S(1)} %bitcast.45), kind=kOutput, calls=%fused_computation.3 | convolution fusion | flops 1208057856 | bytes 6162432 | tf_op jit(solution)/shard_map/dot_general | solution.py:25
  37.6 0.0 all-gather.7.cloned.1.call-update
  37.6 0.0 all-gather.9.cloned.1.call-start
  37.6 4.3 %collective-permute-start = (s32[1,512]{1,0:T(1,128)S(1)}, s32[1,512]{1,0:T(1,128)S(1)}, u32[]{:S(2)}, u32[]{:S(2)}) collective-permute-start(s32[1,512]{1,0:T(1,128)S(1)} %get-tuple-element.19), channel_id=1, source_target_pairs={{4,0},{8,4},{12,8},{16,12},{20,16},{24,20},{28,24},{0,28},{5,1},{9... | collective-permute-start | bytes 6152 | tf_op jit(solution)/shard_map/ppermute | solution.py:21
  41.9 1.3 collective-permute-done
  43.2 14.2 %all-gather.7.cloned.1.call-done = f32[192,2048]{1,0:T(8,128)} async-done(((f32[192,512]{1,0:T(8,128)}), f32[192,2048]{1,0:T(8,128)}) %all-gather.7.cloned.1.call-update) | async-done | bytes 1572880 | tf_op jit(solution)/shard_map/all_gather | solution.py:128
  57.4 0.0 copy-start
  57.4 5.7 %broadcast_multiply_fusion.2 = f32[192,512]{1,0:T(8,128)} fusion(f32[512]{0:T(512)S(1)} %bitcast.46, f32[192,2048]{1,0:T(8,128)} %all-gather.7.cloned.1.call-done, f32[512,2048]{1,0:T(8,128)} %param.4), kind=kOutput, calls=%fused_computation.16 | convolution fusion | flops 1208057856 | bytes 6162432 | tf_op jit(solution)/shard_map/dot_general | solution.py:25
  63.1 0.0 all-gather.9.cloned.1.call-update
  63.2 0.0 all-gather.11.cloned.1.call-start
  63.2 3.9 %collective-permute-start.2 = (s32[1,512]{1,0:T(1,128)S(1)}, s32[1,512]{1,0:T(1,128)S(1)}, u32[]{:S(2)}, u32[]{:S(2)}) collective-permute-start(s32[1,512]{1,0:T(1,128)S(1)} %get-tuple-element.19), channel_id=1, source_target_pairs={{8,0},{12,4},{16,8},{20,12},{24,16},{28,20},{0,24},{4,28},{9,1},{1... | collective-permute-start | bytes 6152 | tf_op jit(solution)/shard_map/ppermute | solution.py:21
  67.1 1.3 collective-permute-done.2
  68.4 0.0 copy-done
  68.5 1.4 fusion.25.gram
  69.9 11.3 %factor.4 = (f32[192,192]{1,0:T(8,128)S(1)}, f32[1,192]{1,0:T(1,128)S(1)}) custom-call(f32[192,192]{1,0:T(8,128)S(1)} %fusion.25.gram), custom_call_target="tpu_custom_call" | custom-call | flops 10000000000 | bytes 442368 | tf_op jit(solution)/shard_map/factor/pallas_call | solution.py:95
  81.2 1.8 all-gather.9.cloned.1.call-done
  83.0 2.8 %fusion.26 = f32[192,2048]{1,0:T(8,128)S(1)} fusion(f32[192,192]{1,0:T(8,128)S(1)} %get-tuple-element.10, f32[192,2048]{1,0:T(8,128)} %all-gather.9.cloned.1.call-done), kind=kOutput, calls=%fused_computation.37 | convolution fusion | flops 905969664 | bytes 3293184 | tf_op jit(solution)/shard_map/dot_general | solution.py:25
  85.9 5.1 %broadcast_multiply_fusion.1 = f32[192,512]{1,0:T(8,128)} fusion(f32[512]{0:T(512)S(1)} %bitcast.43, f32[192,2048]{1,0:T(8,128)S(1)} %fusion.26, f32[512,2048]{1,0:T(8,128)} %param.4), kind=kOutput, calls=%fused_computation.14 | convolution fusion | flops 1208057856 | bytes 6162432 | tf_op jit(solution)/shard_map/dot_general | solution.py:25
  91.0 0.0 all-gather.11.cloned.1.call-update
  91.0 0.0 all-gather.13.cloned.1.call-start
  91.1 3.5 %collective-permute-start.4 = (s32[1,512]{1,0:T(1,128)S(1)}, s32[1,512]{1,0:T(1,128)S(1)}, u32[]{:S(2)}, u32[]{:S(2)}) collective-permute-start(s32[1,512]{1,0:T(1,128)S(1)} %get-tuple-element.19), channel_id=1, source_target_pairs={{12,0},{16,4},{20,8},{24,12},{28,16},{0,20},{4,24},{8,28},{13,1},{... | collective-permute-start | bytes 6152 | tf_op jit(solution)/shard_map/ppermute | solution.py:21
  94.6 1.3 collective-permute-done.4
  95.9 1.4 fusion.27.gram
  97.3 11.3 %factor.5 = (f32[192,192]{1,0:T(8,128)S(1)}, f32[1,192]{1,0:T(1,128)S(1)}) custom-call(f32[192,192]{1,0:T(8,128)S(1)} %fusion.27.gram), custom_call_target="tpu_custom_call" | custom-call | flops 10000000000 | bytes 442368 | tf_op jit(solution)/shard_map/factor/pallas_call | solution.py:95
  108.7 2.2 %all-gather.11.cloned.1.call-done = f32[192,2048]{1,0:T(8,128)} async-done(((f32[192,512]{1,0:T(8,128)}), f32[192,2048]{1,0:T(8,128)}) %all-gather.11.cloned.1.call-update) | async-done | bytes 1572880 | tf_op jit(solution)/shard_map/all_gather | solution.py:128
  110.8 2.8 %fusion.28 = f32[192,2048]{1,0:T(8,128)S(1)} fusion(f32[192,192]{1,0:T(8,128)S(1)} %get-tuple-element.11, f32[192,2048]{1,0:T(8,128)} %all-gather.11.cloned.1.call-done), kind=kOutput, calls=%fused_computation.39 | convolution fusion | flops 905969664 | bytes 3293184 | tf_op jit(solution)/shard_map/dot_general | solution.py:25
  113.7 5.2 %broadcast_multiply_fusion = f32[192,512]{1,0:T(8,128)} fusion(f32[512]{0:T(512)S(1)} %bitcast.44, f32[192,2048]{1,0:T(8,128)S(1)} %fusion.28, f32[512,2048]{1,0:T(8,128)} %param.4), kind=kOutput, calls=%fused_computation.12 | convolution fusion | flops 1208057856 | bytes 6162432 | tf_op jit(solution)/shard_map/dot_general | solution.py:25
  118.9 0.0 all-gather.13.cloned.1.call-update
  118.9 2.3 %convolution_bitcast_fusion.1 = f32[1,192,512]{2,1,0:T(8,128)} fusion(f32[192,2048]{1,0:T(8,128)} %all-gather.7.cloned.1.call-done, s32[]{:T(128)S(6)} %select_n.2, f32[192,192]{1,0:T(8,128)S(1)} %get-tuple-element.10), kind=kOutput, calls=%fused_computation.5 | convolution fusion | flops 226529280 | bytes 933892 | tf_op jit(solution)/shard_map/dot_general | solution.py:25
  121.2 1.6 collective-permute-start.7
  122.7 1.3 fusion.7
  124.0 1.6 collective-permute-start.1
  125.6 1.4 fusion.29.gram
  127.1 11.3 %factor.6 = (f32[192,192]{1,0:T(8,128)S(1)}, f32[1,192]{1,0:T(1,128)S(1)}) custom-call(f32[192,192]{1,0:T(8,128)S(1)} %fusion.29.gram), custom_call_target="tpu_custom_call" | custom-call | flops 10000000000 | bytes 442368 | tf_op jit(solution)/shard_map/factor/pallas_call | solution.py:95
  138.4 0.6 all-gather.13.cloned.1.call-done
  139.0 2.8 %fusion.30 = f32[192,2048]{1,0:T(8,128)S(1)} fusion(f32[192,192]{1,0:T(8,128)S(1)} %get-tuple-element.12, f32[192,2048]{1,0:T(8,128)} %all-gather.13.cloned.1.call-done), kind=kOutput, calls=%fused_computation.41 | convolution fusion | flops 905969664 | bytes 3293184 | tf_op jit(solution)/shard_map/dot_general | solution.py:25
  141.8 1.4 fusion.31
  143.3 2.5 %collective-permute-start.5 = (f32[192,192]{1,0:T(8,128)S(1)}, f32[192,192]{1,0:T(8,128)S(1)}, u32[]{:S(2)}, u32[]{:S(2)}) collective-permute-start(f32[192,192]{1,0:T(8,128)S(1)} %fusion.31), channel_id=1, source_target_pairs={{20,0},{24,4},{28,8},{0,12},{4,16},{8,20},{12,24},{16,28},{21,1},{... | collective-permute-start | bytes 442376 | tf_op jit(solution)/shard_map/ppermute | solution.py:21
  145.8 0.5 fusion.5
  146.3 1.5 collective-permute-start.8
  147.8 1.3 collective-permute-start.3
  149.2 0.0 copy-start.1
  149.2 24.1 %collective-permute-done.5.gram = f32[192,192]{1,0:T(8,128)S(1)} collective-permute-done((f32[192,192]{1,0:T(8,128)S(1)}, f32[192,192]{1,0:T(8,128)S(1)}, u32[]{:S(2)}, u32[]{:S(2)}) %collective-permute-start.5) | collective-permute-done | bytes 147488 | tf_op jit(solution)/shard_map/ppermute | solution.py:21
  173.2 0.2 collective-permute-start.6
  173.5 11.3 %factor.7 = (f32[192,192]{1,0:T(8,128)S(1)}, f32[1,192]{1,0:T(1,128)S(1)}) custom-call(f32[192,192]{1,0:T(8,128)S(1)} %collective-permute-done.5.gram), custom_call_target="tpu_custom_call" | custom-call | flops 10000000000 | bytes 442368 | tf_op jit(solution)/shard_map/factor/pallas_call | solution.py:95
  184.8 0.0 collective-permute-done.7
  184.8 0.0 collective-permute-done.8
  184.8 0.6 maximum_bitcast_fusion.1
  185.4 0.3 collective-permute-done.6
  185.7 0.5 convolution_bitcast_fusion
  186.2 0.0 collective-permute-done.1
  186.2 0.0 collective-permute-done.3
  186.2 0.0 copy-done.1
  186.2 1.3 maximum_bitcast_fusion
  (4 shorter events, 0.1 us)
Async XLA Ops:
  7.2 24.8 %all-gather.15.cloned.1.call-start = ((), (), s32[]{:S(2)}) async-start(), calls=%async_computation.4 | async-start | bytes 1966080 | tf_op jit(solution)/shard_map/all_gather | solution.py:128
  7.9 49.5 %all-gather.7.cloned.1.call-start = ((), (), s32[]{:S(2)}) async-start(), calls=%async_computation | async-start | bytes 1966080 | tf_op jit(solution)/shard_map/all_gather | solution.py:128
  37.6 45.4 %all-gather.9.cloned.1.call-start = ((), (), s32[]{:S(2)}) async-start(), calls=%async_computation.1 | async-start | bytes 1966080 | tf_op jit(solution)/shard_map/all_gather | solution.py:128
  37.6 5.6 %collective-permute-start = (s32[1,512]{1,0:T(1,128)S(1)}, s32[1,512]{1,0:T(1,128)S(1)}, u32[]{:S(2)}, u32[]{:S(2)}) collective-permute-start(s32[1,512]{1,0:T(1,128)S(1)} %get-tuple-element.19), channel_id=1, source_target_pairs={{4,0},{8,4},{12,8},{16,12},{20,16},{24,20},{28,24},{0,28},{5,1},{9... | collective-permute-start | bytes 6152 | tf_op jit(solution)/shard_map/ppermute | solution.py:21
  57.4 11.0 %copy-start = (f32[192,2048]{1,0:T(8,128)S(1)}, f32[192,2048]{1,0:T(8,128)}, u32[]{:S(2)}) copy-start(f32[192,2048]{1,0:T(8,128)} %all-gather.7.cloned.1.call-done) | copy-start | bytes 4718596
  63.2 47.7 %all-gather.11.cloned.1.call-start = ((), (), s32[]{:S(2)}) async-start(), calls=%async_computation.2 | async-start | bytes 1966080 | tf_op jit(solution)/shard_map/all_gather | solution.py:128
  63.2 5.2 %collective-permute-start.2 = (s32[1,512]{1,0:T(1,128)S(1)}, s32[1,512]{1,0:T(1,128)S(1)}, u32[]{:S(2)}, u32[]{:S(2)}) collective-permute-start(s32[1,512]{1,0:T(1,128)S(1)} %get-tuple-element.19), channel_id=1, source_target_pairs={{8,0},{12,4},{16,8},{20,12},{24,16},{28,20},{0,24},{4,28},{9,1},{1... | collective-permute-start | bytes 6152 | tf_op jit(solution)/shard_map/ppermute | solution.py:21
  91.0 47.9 %all-gather.13.cloned.1.call-start = ((), (), s32[]{:S(2)}) async-start(), calls=%async_computation.3 | async-start | bytes 1966080 | tf_op jit(solution)/shard_map/all_gather | solution.py:128
  91.1 4.8 %collective-permute-start.4 = (s32[1,512]{1,0:T(1,128)S(1)}, s32[1,512]{1,0:T(1,128)S(1)}, u32[]{:S(2)}, u32[]{:S(2)}) collective-permute-start(s32[1,512]{1,0:T(1,128)S(1)} %get-tuple-element.19), channel_id=1, source_target_pairs={{12,0},{16,4},{20,8},{24,12},{28,16},{0,20},{4,24},{8,28},{13,1},{... | collective-permute-start | bytes 6152 | tf_op jit(solution)/shard_map/ppermute | solution.py:21
  121.2 63.6 %collective-permute-start.7 = (f32[1,192]{1,0:T(1,128)S(1)}, f32[1,192]{1,0:T(1,128)S(1)}, u32[]{:S(2)}, u32[]{:S(2)}) collective-permute-start(f32[1,192]{1,0:T(1,128)S(1)} %get-tuple-element.15), channel_id=1, source_target_pairs={{28,0},{0,4},{4,8},{8,12},{12,16},{16,20},{20,24},{24,28},{29,1},{... | collective-permute-start | bytes 2312 | tf_op jit(solution)/shard_map/ppermute | solution.py:21
  124.0 62.2 %collective-permute-start.1 = (f32[192,512]{1,0:T(8,128)}, f32[192,512]{1,0:T(8,128)S(1)}, u32[]{:S(2)}, u32[]{:S(2)}) collective-permute-start(f32[192,512]{1,0:T(8,128)} %fusion.7), channel_id=1, source_target_pairs={{28,0},{0,4},{4,8},{8,12},{12,16},{16,20},{20,24},{24,28},{29,1},{... | collective-permute-start | bytes 1179656 | tf_op jit(solution)/shard_map/ppermute | solution.py:21
  143.3 30.0 %collective-permute-start.5 = (f32[192,192]{1,0:T(8,128)S(1)}, f32[192,192]{1,0:T(8,128)S(1)}, u32[]{:S(2)}, u32[]{:S(2)}) collective-permute-start(f32[192,192]{1,0:T(8,128)S(1)} %fusion.31), channel_id=1, source_target_pairs={{20,0},{24,4},{28,8},{0,12},{4,16},{8,20},{12,24},{16,28},{21,1},{... | collective-permute-start | bytes 442376 | tf_op jit(solution)/shard_map/ppermute | solution.py:21
  146.3 38.5 %collective-permute-start.8 = (f32[1,192]{1,0:T(1,128)S(1)}, f32[1,192]{1,0:T(1,128)S(1)}, u32[]{:S(2)}, u32[]{:S(2)}) collective-permute-start(f32[1,192]{1,0:T(1,128)S(1)} %get-tuple-element.16), channel_id=1, source_target_pairs={{24,0},{28,4},{0,8},{4,12},{8,16},{12,20},{16,24},{20,28},{25,1},{... | collective-permute-start | bytes 2312 | tf_op jit(solution)/shard_map/ppermute | solution.py:21
  147.8 38.4 %collective-permute-start.3 = (f32[192,512]{1,0:T(8,128)S(1)}, f32[192,512]{1,0:T(8,128)S(1)}, u32[]{:S(2)}, u32[]{:S(2)}) collective-permute-start(f32[192,512]{1,0:T(8,128)S(1)} %fusion.5), channel_id=1, source_target_pairs={{24,0},{28,4},{0,8},{4,12},{8,16},{12,20},{16,24},{20,28},{25,1},{... | collective-permute-start | bytes 1179656 | tf_op jit(solution)/shard_map/ppermute | solution.py:21
  149.2 37.1 %copy-start.1 = (f32[1,192,512]{2,1,0:T(8,128)S(1)}, f32[1,192,512]{2,1,0:T(8,128)}, u32[]{:S(2)}) copy-start(f32[1,192,512]{2,1,0:T(8,128)} %convolution_bitcast_fusion.1) | copy-start | bytes 1179652
  173.2 12.5 %collective-permute-start.6 = (f32[192,512]{1,0:T(8,128)S(1)}, f32[192,512]{1,0:T(8,128)S(1)}, u32[]{:S(2)}, u32[]{:S(2)}) collective-permute-start(f32[192,512]{1,0:T(8,128)S(1)} %constant_dynamic-slice_fusion), channel_id=1, source_target_pairs={{20,0},{24,4},{28,8},{0,12},{4,16},{8,20},{12,24},{16,28},{21,1},{... | collective-permute-start | bytes 1179656 | tf_op jit(solution)/shard_map/ppermute | solution.py:21
Sparse Core Ops, SparseCore 0:
  9.6 22.3 all-gather.14
  37.7 19.6 all-gather.6
  63.3 19.6 all-gather.8
  91.2 19.6 all-gather.10
  119.0 19.8 all-gather.12

commit v2 on v1

v2 whole, which is shorter than its diff:
```python
import functools
import math

import jax
import jax.numpy as jnp
from jax import lax
from jax.experimental import pallas as pl
from jax.experimental.pallas import tpu as pltpu
from jax.sharding import PartitionSpec as P

coupling = 0.17725
LANES = 128
B = 8


def contract(left, right, dims, precision):
    return lax.dot_general(
        left,
        right,
        (dims, ((), ())),
        precision=precision,
        preferred_element_type=jnp.float32,
    )


HIGHEST = lax.Precision.HIGHEST


def factor_into(work, columns, midway=None):
    r, width = work.shape
    tiles = width // LANES
    lane = lax.broadcasted_iota(jnp.int32, (1, LANES), 1)
    lane_all = lax.broadcasted_iota(jnp.int32, (1, width), 1)
    diagonal = [jnp.ones((1, LANES), jnp.float32) for _ in range(tiles)]
    for p in range(0, r, B):
        if midway is not None and p == (r * 3 // 4) // B * B:
            midway()
        home, off = p // LANES, p % LANES
        block = work[p : p + B, home * LANES : (home + 1) * LANES]
        for j in range(B):
            columns[j * B : (j + 1) * B, :] = jnp.broadcast_to(
                block[:, off + j : off + j + 1], (B, LANES)
            )
        d = [[columns[j * B + i : j * B + i + 1, :] for j in range(i + 1)] for i in range(B)]
        rows = []
        for t in range(B):
            parts = [work[p + t : p + t + 1, q * LANES : (q + 1) * LANES] for q in range(tiles)]
            unit = (lane == off + t).astype(jnp.float32)
            parts[home] = jnp.where((lane >= off) & (lane < off + B), unit, parts[home])
            rows.append(parts)
        for t in range(B):
            inverse = lax.rsqrt(d[t][t])
            diagonal[home] = jnp.where(lane == off + t, inverse, diagonal[home])
            below = [d[s][t] * inverse for s in range(t + 1, B)]
            for s in range(t + 1, B):
                for u in range(t + 1, s + 1):
                    d[s][u] = d[s][u] - below[s - t - 1] * below[u - t - 1]
            rows[t] = [part * inverse for part in rows[t]]
            for s in range(t + 1, B):
                rows[s] = [a - below[s - t - 1] * b for a, b in zip(rows[s], rows[t])]
        for t in range(B):
            for q in range(tiles):
                work[p + t : p + t + 1, q * LANES : (q + 1) * LANES] = rows[t][q]
        if p + B < r:
            pivot = work[p : p + B, :]
            turned = pivot.T[p + B : r, :]
            change = contract(turned, pivot, ((1,), (0,)), HIGHEST)
            rest = work[p + B : r, :]
            rest = jnp.where((lane_all >= p) & (lane_all < p + B), 0.0, rest)
            work[p + B : r, :] = rest - change
    return jnp.concatenate(diagonal, axis=1)


HIGH = lax.Precision.HIGH
MESH = pl.DeviceIdType.MESH


def split(value):
    high = value.astype(jnp.bfloat16)
    return high, (value - high.astype(jnp.float32)).astype(jnp.bfloat16)


def chain_kernel(
    n_tm,
    n_inner,
    hops,
    start,
    kinetic,
    fields,
    orbits,
    logs,
    full,
    panel,
    kin,
    kin_high,
    kin_low,
    scales,
    stage,
    log_stage,
    log_in,
    gram_out,
    gram_in,
    moved,
    inverse,
    work,
    columns,
    ag_send,
    ag_recv,
    far_send,
    far_recv,
    local,
):
    r, rows = start.shape
    sites = n_inner * rows
    chips = n_inner // 2
    gain = math.sqrt(sites)
    last = hops - 1
    tm = lax.axis_index("tm")
    me = lax.axis_index("inner")
    chip, core = me // 2, me % 2
    sibling = chip * 2 + (1 - core)
    across = [((chip + d) % chips) * 2 + core for d in range(1, chips)]
    origin = [((chip + chips - d) % chips) * 2 + core for d in range(1, chips)]

    def ahead(distance):
        return lax.rem(tm + distance + n_tm, n_tm)

    offsets = sorted({d % n_tm for k in range(1, hops) for d in (k, -k)})
    barrier = pltpu.get_barrier_semaphore()
    for peer in [sibling] + across:
        pl.semaphore_signal(barrier, inc=1, device_id={"inner": peer}, device_id_type=MESH)
    for d in offsets:
        pl.semaphore_signal(barrier, inc=1, device_id={"tm": ahead(d)}, device_id_type=MESH)
    load_kin = pltpu.make_async_copy(kinetic, kin, local.at[0])
    load_kin.start()
    load_start = pltpu.make_async_copy(start, full.at[0, me], local.at[1])
    load_start.start()
    own_fields = fields[:, pl.ds(pl.multiple_of(me * rows, rows), rows)]
    scales[0] = jnp.broadcast_to(jnp.exp(coupling * own_fields.astype(jnp.float32)), (8, rows))
    load_start.wait()
    pl.semaphore_wait(barrier, chips + len(offsets))

    def send(source, target, sems, device):
        return pltpu.make_async_remote_copy(
            src_ref=source,
            dst_ref=target,
            send_sem=sems[0],
            recv_sem=sems[1],
            device_id=device,
            device_id_type=MESH,
        )

    def gather(g):
        def sems(i):
            return ag_send.at[g, i], ag_recv.at[g, i]

        def block(slot, i, device):
            return send(full.at[g, slot], full.at[g, slot], sems(i), {"inner": device})

        crossing = [block(me, d, across[d - 1]) for d in range(1, chips)]
        beside = block(me, 0, sibling)
        passed = [block(origin[d - 1], chips - 1 + d, sibling) for d in range(1, chips)]
        for copy in crossing:
            copy.start()
        beside.start()

        def forward():
            for copy, onward in zip(crossing, passed):
                copy.wait_recv()
                onward.start()

        def finish():
            beside.wait()
            for copy in crossing:
                copy.wait_send()
            for copy in passed:
                copy.wait()

        return forward, finish

    def far(kind, k):
        return far_send.at[kind, k], far_recv.at[kind, k]

    def mapped(blocks, hop):
        total = jnp.zeros((r, rows), jnp.float32)
        for j in range(n_inner):
            high, low = split(blocks[j])
            dims = ((1,), (0,))
            total += contract(high, kin_high[j], dims, None)
            total += contract(high, kin_low[j], dims, None)
            total += contract(low, kin_high[j], dims, None)
        return total * scales[hop][0:1, :]

    def gram_of(blocks):
        total = jnp.zeros((r, r), jnp.float32)
        for j in range(n_inner):
            block = blocks[j]
            total += contract(block, block, ((1,), (1,)), HIGHEST)
        return total

    below = lax.broadcasted_iota(jnp.int32, (r, r), 0) >= lax.broadcasted_iota(
        jnp.int32, (r, r), 1
    )

    def factor(midway=None):
        diagonal = factor_into(work, columns, midway)
        inverse[...] = jnp.where(below, work[:, :r], 0.0)
        return -jnp.log(diagonal)

    pending = []
    forward, finish = gather(0)
    for k in range(1, hops):
        copy = send(scales.at[0], scales.at[k], far(0, k), {"tm": ahead(-k)})
        copy.start()
        pending.append(copy)
    load_kin.wait()
    for j in range(n_inner):
        turned = kin[:, j * rows : (j + 1) * rows].T
        kin_high[j], kin_low[j] = split(turned)
    forward()
    finish()
    full[1, me] = mapped(full.at[0], 0)
    forward, finish = gather(1)
    for copy in pending:
        copy.wait()
    pending = []
    forward()
    finish()

    blocks = full.at[1]
    work[...] = jnp.zeros_like(work)
    for hop in range(hops):
        if hop < last:
            full[hop + 2, me] = mapped(blocks, hop + 1)
            forward, finish = gather(hop + 2)
            work[:, :r] = gram_of(blocks)
            log_stage[hop] = jnp.broadcast_to(factor(forward), log_stage.shape[1:])
            stage[hop] = contract(gain * inverse[...], blocks[me], ((1,), (0,)), HIGH)
            if hop == 0:
                copy = pltpu.make_async_copy(stage.at[0], orbits.at[0], local.at[2])
                copy.start()
                pending.append(copy)
            else:
                there = {"tm": ahead(hop)}
                copy = send(stage.at[hop], orbits.at[hop], far(1, hop), there)
                copy.start()
                pending.append(copy)
                copy = send(log_stage.at[hop], log_in.at[hop], far(2, hop), there)
                copy.start()
                pending.append(copy)
            finish()
            for j in range(n_inner):
                panel[j] = contract(inverse[...], full[hop + 2, j], ((1,), (0,)), HIGH)
            blocks = panel
        else:
            there = {"tm": ahead(last)}
            half = r // 2
            part = pl.ds(pl.multiple_of(core * half, 8), half)
            gram_out[:, :r] = gram_of(blocks)
            gram_out[:, r:] = jnp.zeros((r, gram_out.shape[1] - r), jnp.float32)
            shift = send(gram_out.at[part], gram_in.at[part], far(3, 0), there)
            shift.start()
            carry = send(panel.at[me], moved, far(3, 1), there)
            carry.start()
            shift.wait_recv()
            swap = send(gram_in.at[part], gram_in.at[part], far(3, 2), {"inner": sibling})
            swap.start()
            swap.wait()
            work[...] = gram_in[...]
            log_stage[hop] = jnp.broadcast_to(factor(), log_stage.shape[1:])
            shift.wait_send()
            carry.wait()
            stage[hop] = contract(gain * inverse[...], moved[...], ((1,), (0,)), HIGH)
            copy = pltpu.make_async_copy(stage.at[hop], orbits.at[hop], local.at[3])
            copy.start()
            pending.append(copy)
    for copy in pending:
        copy.wait()
    for hop in range(hops):
        held = log_stage if hop in (0, last) else log_in
        logs[hop : hop + 1, :] = held[hop][0:1, :r]


def on_device(start_panels, kinetic, fields):
    rows, sites = kinetic.shape
    r = start_panels.shape[1]
    n_tm, n_inner = lax.axis_size("tm"), lax.axis_size("inner")
    hops = n_tm // 2
    width = -(-r // LANES) * LANES
    f32, bf16 = jnp.float32, jnp.bfloat16
    vmem, anywhere = pl.BlockSpec(memory_space=pltpu.VMEM), pl.BlockSpec(memory_space=pl.ANY)
    orbits, logs = pl.pallas_call(
        functools.partial(chain_kernel, n_tm, n_inner, hops),
        out_shape=(
            jax.ShapeDtypeStruct((hops, r, rows), f32),
            jax.ShapeDtypeStruct((hops, r), f32),
        ),
        in_specs=[anywhere, anywhere, vmem],
        out_specs=(anywhere, vmem),
        scratch_shapes=[
            pltpu.VMEM((hops + 1, n_inner, r, rows), f32),
            pltpu.VMEM((n_inner, r, rows), f32),
            pltpu.VMEM((rows, sites), f32),
            pltpu.VMEM((n_inner, rows, rows), bf16),
            pltpu.VMEM((n_inner, rows, rows), bf16),
            pltpu.VMEM((hops, 8, rows), f32),
            pltpu.VMEM((hops, r, rows), f32),
            pltpu.VMEM((hops, 8, width), f32),
            pltpu.VMEM((hops, 8, width), f32),
            pltpu.VMEM((r, width), f32),
            pltpu.VMEM((r, width), f32),
            pltpu.VMEM((r, rows), f32),
            pltpu.VMEM((r, r), f32),
            pltpu.VMEM((r, width), f32),
            pltpu.VMEM((B * B, LANES), f32),
            pltpu.SemaphoreType.DMA((hops + 1, n_inner)),
            pltpu.SemaphoreType.DMA((hops + 1, n_inner)),
            pltpu.SemaphoreType.DMA((4, max(hops, 3))),
            pltpu.SemaphoreType.DMA((4, max(hops, 3))),
            pltpu.SemaphoreType.DMA((4,)),
        ],
        compiler_params=pltpu.CompilerParams(
            collective_id=0, has_side_effects=True, vmem_limit_bytes=48 * 2**20
        ),
        name="chain",
    )(start_panels[0], kinetic, fields)
    return orbits[None], logs[None]


def solution(mesh):
    placed = (P("tm", None, "inner"), P("inner", None), P("tm", None))
    return jax.shard_map(
        on_device,
        mesh=mesh,
        in_specs=placed,
        out_specs=(P("tm", None, None, "inner"), P("tm", None, None)),
        check_vma=False,
    )
```

time: 198 us -> 123 us (0.62); the launches traced: 194 us -> 123 us
  Pallas kernels: 45.3 us -> 117 us
  waiting for transfers between devices: 71 us -> 0 us
  matrix products: 40.5 us -> 0 us
  starting transfers between devices: 20.7 us -> 0 us
  between operations: 14.2 us -> 0.65 us
  local copies, waits for them, and re-layouts: 0.03 us -> 5.61 us
  other arithmetic: 2.62 us -> 0 us
    pallas_call x4 -> x1, Pallas kernels: 45.3 us -> 117 us  [on_device(): pl.pallas_call(functools.partial(chain_kernel, n_tm, n_inner, hops), out_...]
    all_gather x5 -> x0, waiting for transfers between devices: 42 us -> none  [gathered(): return lax.all_gather(block, 'inner', axis=1, tiled=True)]
    dot_general x15 -> x0, matrix products: 40.5 us -> none  [contract(): lax.dot_general(left, right, (dims, ((), ())), precision=precision, prefe...]
    ppermute x9 -> x0, waiting for transfers between devices: 28.3 us -> none  [from_behind(): lax.ppermute(block, axis, [((i - distance) % n, i) for i in range(n)])]
    ppermute x9 -> x0, starting transfers between devices: 20.5 us -> none  [from_behind(): lax.ppermute(block, axis, [((i - distance) % n, i) for i in range(n)])]
    unnamed x4 -> x8, local copies, waits for them, and re-layouts: 0.01 us -> 5.61 us
  transfers between devices with their start and end apart: 14 -> 0, of which waited for: 10 -> 0; matrix products, arithmetic and copies ran while one was open for 7% -> 0% of each run, Pallas kernels for 23% -> 0%
where the time goes in v2:
time: 123 us
  Pallas kernels  117 us (95%)
  local copies, waits for them, and re-layouts  5.61 us (5%)
    pallas_call x1, Pallas kernels, on_device(): pl.pallas_call(functools.partial(chain_kernel, n_tm, n_inner, hops), out_...  117 us
    unnamed x8, local copies, waits for them, and re-layouts  5.61 us

profile of v2, /device:TPU:0, one launch (start us, length us, event | category | flops | bytes accessed | tf_op | source)
XLA Modules:
  0.0 122.8 jit_solution(5589145444089639222)
XLA Ops:
  0.6 0.0 copy-start
  0.6 2.2 %copy-done = f32[512,2048]{1,0:T(8,128)S(1)} copy-done((f32[512,2048]{1,0:T(8,128)S(1)}, f32[512,2048]{1,0:T(8,128)}, u32[]{:S(2)}) %copy-start) | copy-done | bytes 4194328
  2.8 0.0 copy-start.1
  2.8 1.0 copy-done.1
  3.8 0.0 copy-start.2
  3.8 0.7 copy-done.2
  4.5 116.5 %chain.1 = (f32[4,192,512]{2,1,0:T(8,128)S(1)}, f32[4,192]{1,0:T(4,128)S(1)}) custom-call(f32[192,512]{1,0:T(8,128)S(1)} %bitcast.4, f32[512,2048]{1,0:T(8,128)S(1)} %copy-done, s32[1,2048]{1,0:T(1,128)S(1)} %copy-done.2), custom_call_target="tpu_custom_call" | custom-call | tf_op jit(solution)/shard_map/chain/pallas_call | solution.py:292
  121.0 1.1 copy.7
  122.2 0.6 copy.8
Async XLA Ops:
  0.6 2.2 %copy-start = (f32[512,2048]{1,0:T(8,128)S(1)}, f32[512,2048]{1,0:T(8,128)}, u32[]{:S(2)}) copy-start(f32[512,2048]{1,0:T(8,128)} %kinetic.1) | copy-start | bytes 12582916
  2.8 1.0 copy-start.1
  3.8 0.7 copy-start.2

commit v3 on v2

--- a/solution.py
+++ b/solution.py
@@ -26,6 +26,13 @@
 HIGHEST = lax.Precision.HIGHEST
 
 
+def split_three(value):
+    f32 = jnp.float32
+    high = value.astype(jnp.bfloat16).astype(f32)
+    middle = (value - high).astype(jnp.bfloat16).astype(f32)
+    return high, middle, value - high - middle
+
+
 def factor_into(work, columns, midway=None):
     r, width = work.shape
     tiles = width // LANES
@@ -33,7 +40,7 @@
     lane_all = lax.broadcasted_iota(jnp.int32, (1, width), 1)
     diagonal = [jnp.ones((1, LANES), jnp.float32) for _ in range(tiles)]
     for p in range(0, r, B):
-        if midway is not None and p == (r * 3 // 4) // B * B:
+        if midway is not None and p == (r * 7 // 8) // B * B:
             midway()
         home, off = p // LANES, p % LANES
         block = work[p : p + B, home * LANES : (home + 1) * LANES]
@@ -63,8 +70,13 @@
                 work[p + t : p + t + 1, q * LANES : (q + 1) * LANES] = rows[t][q]
         if p + B < r:
             pivot = work[p : p + B, :]
-            turned = pivot.T[p + B : r, :]
-            change = contract(turned, pivot, ((1,), (0,)), HIGHEST)
+            high, middle, low = split_three(pivot)
+            left = jnp.concatenate([high, high, middle, high, middle, low], axis=0)
+            right = jnp.concatenate([high, middle, high, low, middle, high], axis=0)
+            begin = (p + B) // 16 * 16
+            turned = left.T[begin:r, :].astype(jnp.bfloat16)
+            change = contract(turned, right.astype(jnp.bfloat16), ((1,), (0,)), None)
+            change = change[p + B - begin :, :]
             rest = work[p + B : r, :]
             rest = jnp.where((lane_all >= p) & (lane_all < p + B), 0.0, rest)
             work[p + B : r, :] = rest - change
@@ -86,7 +98,7 @@
     hops,
     start,
     kinetic,
-    fields,
+    fields_far,
     orbits,
     logs,
     full,
@@ -94,14 +106,14 @@
     kin,
     kin_high,
     kin_low,
+    fields,
     scales,
     stage,
     log_stage,
     log_in,
-    gram_out,
-    gram_in,
     moved,
     inverse,
+    inverse_in,
     work,
     columns,
     ag_send,
@@ -135,6 +147,9 @@
     load_kin.start()
     load_start = pltpu.make_async_copy(start, full.at[0, me], local.at[1])
     load_start.start()
+    load_fields = pltpu.make_async_copy(fields_far, fields, local.at[2])
+    load_fields.start()
+    load_fields.wait()
     own_fields = fields[:, pl.ds(pl.multiple_of(me * rows, rows), rows)]
     scales[0] = jnp.broadcast_to(jnp.exp(coupling * own_fields.astype(jnp.float32)), (8, rows))
     load_start.wait()
@@ -198,14 +213,12 @@
             total += contract(block, block, ((1,), (1,)), HIGHEST)
         return total
 
-    below = lax.broadcasted_iota(jnp.int32, (r, r), 0) >= lax.broadcasted_iota(
-        jnp.int32, (r, r), 1
+    below = lax.broadcasted_iota(jnp.int32, work.shape, 0) >= lax.broadcasted_iota(
+        jnp.int32, work.shape, 1
     )
 
-    def factor(midway=None):
-        diagonal = factor_into(work, columns, midway)
-        inverse[...] = jnp.where(below, work[:, :r], 0.0)
-        return -jnp.log(diagonal)
+    half = r // 2
+    part = pl.ds(pl.multiple_of(core * half, 8), half)
 
     pending = []
     forward, finish = gather(0)
@@ -229,55 +242,57 @@
 
     blocks = full.at[1]
     work[...] = jnp.zeros_like(work)
+    carried, shifted, told, swaps = [], [], [], []
     for hop in range(hops):
+        there = {"tm": ahead(hop)}
         if hop < last:
             full[hop + 2, me] = mapped(blocks, hop + 1)
             forward, finish = gather(hop + 2)
-            work[:, :r] = gram_of(blocks)
-            log_stage[hop] = jnp.broadcast_to(factor(forward), log_stage.shape[1:])
-            stage[hop] = contract(gain * inverse[...], blocks[me], ((1,), (0,)), HIGH)
-            if hop == 0:
-                copy = pltpu.make_async_copy(stage.at[0], orbits.at[0], local.at[2])
-                copy.start()
-                pending.append(copy)
-            else:
-                there = {"tm": ahead(hop)}
-                copy = send(stage.at[hop], orbits.at[hop], far(1, hop), there)
-                copy.start()
-                pending.append(copy)
-                copy = send(log_stage.at[hop], log_in.at[hop], far(2, hop), there)
-                copy.start()
-                pending.append(copy)
+        if hop > 0:
+            stage[hop] = blocks[me]
+            carried.append(send(stage.at[hop], moved.at[hop], far(1, hop), there))
+            carried[-1].start()
+        work[:, :r] = gram_of(blocks)
+        diagonal = factor_into(work, columns, forward if hop < last else None)
+        inverse[hop] = jnp.where(below, work[...], 0.0)
+        log_stage[hop] = jnp.broadcast_to(-jnp.log(diagonal), log_stage.shape[1:])
+        if hop > 0:
+            source, target = inverse.at[hop, part], inverse_in.at[hop, part]
+            shifted.append(send(source, target, far(2, hop), there))
+            shifted[-1].start()
+            told.append(send(log_stage.at[hop], log_in.at[hop], far(3, hop), there))
+            told[-1].start()
+        if hop < last:
             finish()
             for j in range(n_inner):
-                panel[j] = contract(inverse[...], full[hop + 2, j], ((1,), (0,)), HIGH)
+                panel[j] = contract(
+                    inverse[hop][:, :r], full[hop + 2, j], ((1,), (0,)), HIGH
+                )
             blocks = panel
-        else:
-            there = {"tm": ahead(last)}
-            half = r // 2
-            part = pl.ds(pl.multiple_of(core * half, 8), half)
-            gram_out[:, :r] = gram_of(blocks)
-            gram_out[:, r:] = jnp.zeros((r, gram_out.shape[1] - r), jnp.float32)
-            shift = send(gram_out.at[part], gram_in.at[part], far(3, 0), there)
-            shift.start()
-            carry = send(panel.at[me], moved, far(3, 1), there)
-            carry.start()
-            shift.wait_recv()
-            swap = send(gram_in.at[part], gram_in.at[part], far(3, 2), {"inner": sibling})
-            swap.start()
-            swap.wait()
-            work[...] = gram_in[...]
-            log_stage[hop] = jnp.broadcast_to(factor(), log_stage.shape[1:])
-            shift.wait_send()
-            carry.wait()
-            stage[hop] = contract(gain * inverse[...], moved[...], ((1,), (0,)), HIGH)
-            copy = pltpu.make_async_copy(stage.at[hop], orbits.at[hop], local.at[3])
-            copy.start()
-            pending.append(copy)
-    for copy in pending:
+    writes = []
+
+    def write(hop, factor, block):
+        moved[hop] = contract(gain * factor[:, :r], block, ((1,), (0,)), HIGH)
+        writes.append(pltpu.make_async_copy(moved.at[hop], orbits.at[hop], local.at[3 + hop]))
+        writes[-1].start()
+
+    write(0, inverse[0], full[1, me])
+    for group in (range(1, last), range(max(last, 1), hops)):
+        for hop in group:
+            shifted[hop - 1].wait_recv()
+            half_in = inverse_in.at[hop, part]
+            swaps.append(send(half_in, half_in, far(4, hop), {"inner": sibling}))
+            swaps[-1].start()
+        for hop in group:
+            swaps[hop - 1].wait()
+            carried[hop - 1].wait()
+            write(hop, inverse_in[hop], moved[hop])
+    for copy in shifted:
+        copy.wait_send()
+    for copy in told + writes:
         copy.wait()
     for hop in range(hops):
-        held = log_stage if hop in (0, last) else log_in
+        held = log_stage if hop == 0 else log_in
         logs[hop : hop + 1, :] = held[hop][0:1, :r]
 
 
@@ -288,39 +303,39 @@
     hops = n_tm // 2
     width = -(-r // LANES) * LANES
     f32, bf16 = jnp.float32, jnp.bfloat16
-    vmem, anywhere = pl.BlockSpec(memory_space=pltpu.VMEM), pl.BlockSpec(memory_space=pl.ANY)
+    vmem, far = pl.BlockSpec(memory_space=pltpu.VMEM), pl.BlockSpec(memory_space=pltpu.HBM)
     orbits, logs = pl.pallas_call(
         functools.partial(chain_kernel, n_tm, n_inner, hops),
         out_shape=(
             jax.ShapeDtypeStruct((hops, r, rows), f32),
             jax.ShapeDtypeStruct((hops, r), f32),
         ),
-        in_specs=[anywhere, anywhere, vmem],
-        out_specs=(anywhere, vmem),
+        in_specs=[far, far, far],
+        out_specs=(far, vmem),
         scratch_shapes=[
             pltpu.VMEM((hops + 1, n_inner, r, rows), f32),
             pltpu.VMEM((n_inner, r, rows), f32),
             pltpu.VMEM((rows, sites), f32),
             pltpu.VMEM((n_inner, rows, rows), bf16),
             pltpu.VMEM((n_inner, rows, rows), bf16),
+            pltpu.VMEM((1, sites), jnp.int32),
             pltpu.VMEM((hops, 8, rows), f32),
             pltpu.VMEM((hops, r, rows), f32),
             pltpu.VMEM((hops, 8, width), f32),
             pltpu.VMEM((hops, 8, width), f32),
-            pltpu.VMEM((r, width), f32),
-            pltpu.VMEM((r, width), f32),
-            pltpu.VMEM((r, rows), f32),
-            pltpu.VMEM((r, r), f32),
+            pltpu.VMEM((hops, r, rows), f32),
+            pltpu.VMEM((hops, r, width), f32),
+            pltpu.VMEM((hops, r, width), f32),
             pltpu.VMEM((r, width), f32),
             pltpu.VMEM((B * B, LANES), f32),
             pltpu.SemaphoreType.DMA((hops + 1, n_inner)),
             pltpu.SemaphoreType.DMA((hops + 1, n_inner)),
-            pltpu.SemaphoreType.DMA((4, max(hops, 3))),
-            pltpu.SemaphoreType.DMA((4, max(hops, 3))),
-            pltpu.SemaphoreType.DMA((4,)),
+            pltpu.SemaphoreType.DMA((5, hops)),
+            pltpu.SemaphoreType.DMA((5, hops)),
+            pltpu.SemaphoreType.DMA((3 + hops,)),
         ],
         compiler_params=pltpu.CompilerParams(
-            collective_id=0, has_side_effects=True, vmem_limit_bytes=48 * 2**20
+            collective_id=0, has_side_effects=True, vmem_limit_bytes=56 * 2**20
         ),
         name="chain",
     )(start_panels[0], kinetic, fields)

time: 123 us -> 108 us (0.88)
  Pallas kernels: 117 us -> 104 us
  local copies, waits for them, and re-layouts: 5.61 us -> 3.27 us
    pallas_call x1, Pallas kernels: 117 us -> 104 us  [on_device(): pl.pallas_call(functools.partial(chain_kernel, n_tm, n_inner, hops), out_...]
    unnamed x8 -> x4, local copies, waits for them, and re-layouts: 5.61 us -> 3.27 us
where the time goes in v3:
time: 108 us
  Pallas kernels  104 us (96%)
  local copies, waits for them, and re-layouts  3.27 us (3%)
    pallas_call x1, Pallas kernels, on_device(): pl.pallas_call(functools.partial(chain_kernel, n_tm, n_inner, hops), out_...  104 us
    unnamed x4, local copies, waits for them, and re-layouts  3.27 us

profile of v3, /device:TPU:0, one launch (start us, length us, event | category | flops | bytes accessed | tf_op | source)
XLA Modules:
  0.0 108.1 jit_solution(10752255001641838708)
XLA Ops:
  0.6 104.2 %chain.1 = (f32[4,192,512]{2,1,0:T(8,128)}, f32[4,192]{1,0:T(4,128)}) custom-call(f32[192,512]{1,0:T(8,128)} %bitcast.4, f32[512,2048]{1,0:T(8,128)} %kinetic.1, s32[1,2048]{1,0:T(1,128)} %fields_far.1), custom_call_target="tpu_custom_call" | custom-call | tf_op jit(solution)/shard_map/chain/pallas_call | solution.py:307
  104.8 0.0 copy-start
  104.8 2.7 %copy.7 = f32[1,4,192,512]{3,2,1,0:T(8,128)} copy(f32[1,4,192,512]{3,2,1,0:T(8,128)} %bitcast.3) | data formatting | bytes 3145728
  107.5 0.0 copy-done
  107.5 0.6 copy.8
Async XLA Ops:
  104.8 2.7 %copy-start = (f32[4,192]{1,0:T(4,128)S(1)}, f32[4,192]{1,0:T(4,128)}, u32[]{:S(2)}) copy-start(f32[4,192]{1,0:T(4,128)} %get-tuple-element.5) | copy-start | bytes 9220

commit v4 on v3

--- a/solution.py
+++ b/solution.py
@@ -185,26 +185,29 @@
                 onward.start()
 
         def finish():
-            beside.wait()
+            beside.wait_send()
             for copy in crossing:
                 copy.wait_send()
             for copy in passed:
                 copy.wait()
 
-        return forward, finish
+        return beside.wait_recv, forward, finish
 
     def far(kind, k):
         return far_send.at[kind, k], far_recv.at[kind, k]
 
-    def mapped(blocks, hop):
+    def mapped_sum(blocks, order):
         total = jnp.zeros((r, rows), jnp.float32)
-        for j in range(n_inner):
+        for j in order:
             high, low = split(blocks[j])
             dims = ((1,), (0,))
             total += contract(high, kin_high[j], dims, None)
             total += contract(high, kin_low[j], dims, None)
             total += contract(low, kin_high[j], dims, None)
-        return total * scales[hop][0:1, :]
+        return total
+
+    def mapped(blocks, hop):
+        return mapped_sum(blocks, range(n_inner)) * scales[hop][0:1, :]
 
     def gram_of(blocks):
         total = jnp.zeros((r, r), jnp.float32)
@@ -221,7 +224,7 @@
     part = pl.ds(pl.multiple_of(core * half, 8), half)
 
     pending = []
-    forward, finish = gather(0)
+    near, forward, finish = gather(0)
     for k in range(1, hops):
         copy = send(scales.at[0], scales.at[k], far(0, k), {"tm": ahead(-k)})
         copy.start()
@@ -230,13 +233,17 @@
     for j in range(n_inner):
         turned = kin[:, j * rows : (j + 1) * rows].T
         kin_high[j], kin_low[j] = split(turned)
+    near()
+    total = mapped_sum(full.at[0], [me, sibling])
     forward()
     finish()
-    full[1, me] = mapped(full.at[0], 0)
-    forward, finish = gather(1)
+    rest = [c * 2 + u for c in [lax.rem(chip + d, chips) for d in range(1, chips)] for u in (0, 1)]
+    full[1, me] = (total + mapped_sum(full.at[0], rest)) * scales[0][0:1, :]
+    near, forward, finish = gather(1)
     for copy in pending:
         copy.wait()
     pending = []
+    near()
     forward()
     finish()
 
@@ -247,7 +254,7 @@
         there = {"tm": ahead(hop)}
         if hop < last:
             full[hop + 2, me] = mapped(blocks, hop + 1)
-            forward, finish = gather(hop + 2)
+            near, forward, finish = gather(hop + 2)
         if hop > 0:
             stage[hop] = blocks[me]
             carried.append(send(stage.at[hop], moved.at[hop], far(1, hop), there))
@@ -263,6 +270,7 @@
             told.append(send(log_stage.at[hop], log_in.at[hop], far(3, hop), there))
             told[-1].start()
         if hop < last:
+            near()
             finish()
             for j in range(n_inner):
                 panel[j] = contract(
@@ -311,7 +319,7 @@
             jax.ShapeDtypeStruct((hops, r), f32),
         ),
         in_specs=[far, far, far],
-        out_specs=(far, vmem),
+        out_specs=(pl.BlockSpec(memory_space=pl.ANY), vmem),
         scratch_shapes=[
             pltpu.VMEM((hops + 1, n_inner, r, rows), f32),
             pltpu.VMEM((n_inner, r, rows), f32),

time: 108 us -> 108 us (level)
  no operation moved by 1% of the time
where the time goes in v4:
time: 108 us; the launch traced here: 107 us
  Pallas kernels  104 us (96%)
  local copies, waits for them, and re-layouts  3.27 us (3%)
    pallas_call x1, Pallas kernels, on_device(): pl.pallas_call(functools.partial(chain_kernel, n_tm, n_inner, hops), out_...  104 us
    unnamed x4, local copies, waits for them, and re-layouts  3.27 us

profile of v4, /device:TPU:0, one launch (start us, length us, event | category | flops | bytes accessed | tf_op | source)
XLA Modules:
  0.0 107.5 jit_solution(9667279693851678108)
XLA Ops:
  0.6 103.6 %chain.1 = (f32[4,192,512]{2,1,0:T(8,128)}, f32[4,192]{1,0:T(4,128)}) custom-call(f32[192,512]{1,0:T(8,128)} %bitcast.4, f32[512,2048]{1,0:T(8,128)} %kinetic.1, s32[1,2048]{1,0:T(1,128)} %fields_far.1), custom_call_target="tpu_custom_call" | custom-call | tf_op jit(solution)/shard_map/chain/pallas_call | solution.py:315
  104.2 0.0 copy-start
  104.2 2.7 %copy.7 = f32[1,4,192,512]{3,2,1,0:T(8,128)} copy(f32[1,4,192,512]{3,2,1,0:T(8,128)} %bitcast.3) | data formatting | bytes 3145728
  106.9 0.0 copy-done
  106.9 0.6 copy.8
Async XLA Ops:
  104.2 2.7 %copy-start = (f32[4,192]{1,0:T(4,128)S(1)}, f32[4,192]{1,0:T(4,128)}, u32[]{:S(2)}) copy-start(f32[4,192]{1,0:T(4,128)} %get-tuple-element.5) | copy-start | bytes 9220
